TPU v7x, 32 devices: a whole 2x2x4 slice. The times are simulated.
32 devices in a mesh: mp: 8 (over z, x), seq: 4 (over y, core).
Axes of the slice: x: 2, y: 2, z: 4, core: 2. Of those that a mesh axis runs over, the one named last changes fastest.
Arguments:
- hidden_in: bfloat16 [256, 8192], P(None, 'mp'), may hold values from -4 to 4
- attn_gain: bfloat16 [8192], P('mp'), may hold values from 0.099609375 to 1.8984375
- mlp_gain: bfloat16 [8192], replicated, may hold values from 0.099609375 to 1.8984375
- w_query: bfloat16 [8192, 8192], P('mp', 'seq'), may hold values from -1 to 1
- w_key: bfloat16 [8192, 1024], P('mp', 'seq'), may hold values from -1 to 1
- w_value: bfloat16 [8192, 1024], P('mp', 'seq'), may hold values from -0.0625 to 0.0625
- w_out: bfloat16 [8192, 8192], P('seq', 'mp'), may hold values from -0.0625 to 0.0625
- w_gate: bfloat16 [8192, 28672], P(None, ('mp', 'seq')), may hold values from -0.0625 to 0.0625
- w_up: bfloat16 [8192, 28672], P(None, ('mp', 'seq')), may hold values from -0.0625 to 0.0625
- w_down: bfloat16 [28672, 8192], P(('mp', 'seq')), may hold values from -0.03125 to 0.03125
- prompt_cache: bfloat16 [8, 8, 32768, 256], P(None, 'seq', 'mp'), may hold values from -136 to 136
- tail_cache: bfloat16 [128, 8, 512, 256], P('mp', 'seq'), may hold values from -136 to 136
- prompt_len: int32 [8], replicated, may hold values from 4096 to 32768, as said below
- tail_len: int32 [128], replicated, may hold values from 1 to 512, as said below
- prompt_of: int32 [128], replicated, may hold values from 0 to 7, as said below
Outputs:
- layer_out: bfloat16 [256, 8192], P(('mp', 'seq'))
- input_rms: float32 [256], replicated
- max_logit: float32 [128, 64], P(None, 'seq')
- new_entries: bfloat16 [128, 8, 2, 256], P('mp', 'seq')
Inputs may be any that keep to these rules, and one draw needn't show every extreme that they name: `prompt_len`: at least one prompt has 32768 positions. `tail_len`: at least one request has 512 tail positions. `prompt_of`: each prompt feeds exactly 16 requests.
All inputs are finite; a program needn't handle non-finite values.
Results may differ from a plain program's by a relative error of at most 0.028.
The roundings to bfloat16 on the way count: a program that leaves them out, or rounds other values in their place, can miss the bound.
Values may be sent and summed in bfloat16 or wider, within the bound.
A program may use at most 320 MiB of HBM per device.

v0:
```python
import jax
import jax.numpy as jnp
from jax import lax
from jax.sharding import PartitionSpec as P

D = 8192
HD = 128
PROMPTS = 8
CONT = 16
QPK = 8
REQ = 128
EPS = 1e-05
THETA = 500000.0
NEG = -1e30


def joined(part, axis, combine):
    gathered = jax.tree.map(lambda a: lax.all_gather(a, axis), part)

    def take(source):
        return jax.tree.map(lambda a: lax.dynamic_index_in_dim(a, source, 0, False), gathered)

    return lax.fori_loop(
        1, lax.axis_size(axis), lambda source, state: combine(state, take(source)), take(0)
    )


def rope_table(position, head_dim):
    half_width = head_dim // 2
    frequency = THETA ** (-(jnp.arange(half_width, dtype=jnp.float32) * 2.0 / head_dim))
    rotation = position.astype(jnp.float32)[:, None] * frequency[None, :]
    return (jnp.cos(rotation), jnp.sin(rotation))


def apply_rope(vectors, cosine, sine_table):
    half_width = vectors.shape[-1] // 2
    first_half = vectors[..., :half_width]
    second_half = vectors[..., half_width:]
    cos_rows = cosine[:, None, :]
    sin_rows = sine_table[:, None, :]
    return jnp.concatenate(
        [
            first_half * cos_rows - second_half * sin_rows,
            second_half * cos_rows + first_half * sin_rows,
        ],
        axis=-1,
    )


def merge_partials(earlier, later):
    top_early, total_early, accum_early = earlier
    top_late, total_late, accum_late = later
    highest = jnp.maximum(top_early, top_late)
    factor_early = jnp.exp(top_early - highest)
    factor_late = jnp.exp(top_late - highest)
    return (
        highest,
        total_early * factor_early + total_late * factor_late,
        accum_early * factor_early[..., None] + accum_late * factor_late[..., None],
    )


def softmax_terms(scores, valid_mask):
    masked = jnp.where(valid_mask, scores, NEG)
    highest = jnp.max(masked, axis=-1)
    weights = jnp.where(valid_mask, jnp.exp(masked - highest[..., None]), 0.0)
    return (highest, jnp.sum(weights, axis=-1), weights.astype(jnp.bfloat16))


def prompt_terms(queries, cache_block, lengths, first_place):
    head_dim = queries.shape[-1]
    keys_block = cache_block[..., :head_dim]
    values_block = cache_block[..., head_dim:]
    scores = jnp.einsum(
        "pntgqd,pgjd->pntgqj", queries, keys_block, preferred_element_type=jnp.float32
    ) * head_dim ** (-0.5)
    places = first_place + jnp.arange(cache_block.shape[2], dtype=jnp.int32)
    valid_mask = (places[None, :] < lengths[:, None])[:, None, None, None, None, :]
    highest, totals, weights = softmax_terms(scores, valid_mask)
    accum = jnp.einsum(
        "pntgqj,pgjd->pntgqd", weights, values_block, preferred_element_type=jnp.float32
    )
    return (highest, totals, accum)


def shards(
    hidden_in,
    attn_gain,
    mlp_gain,
    w_query,
    w_key,
    w_value,
    w_out,
    w_gate,
    w_up,
    w_down,
    prompt_cache,
    tail_cache,
    prompt_len,
    tail_len,
    prompt_of,
):
    model_index = lax.axis_index("mp")
    seq_index = lax.axis_index("seq")
    model_count = lax.axis_size("mp")
    seq_count = lax.axis_size("seq")
    row_total = hidden_in.shape[0]
    kv_local = prompt_cache.shape[1]
    local_span = prompt_cache.shape[2]
    head_local = w_query.shape[1] // HD
    req_local = tail_cache.shape[0]
    tail_span = tail_cache.shape[2]
    row_share = row_total // (model_count * seq_count)
    score_scale = HD ** (-0.5)
    wide_in = hidden_in.astype(jnp.float32)
    scaled_in = (wide_in * attn_gain.astype(jnp.float32)[None, :]).astype(jnp.bfloat16)
    query_part = jnp.dot(scaled_in, w_query, preferred_element_type=jnp.float32)
    key_part = jnp.dot(scaled_in, w_key, preferred_element_type=jnp.float32)
    value_part = jnp.dot(scaled_in, w_value, preferred_element_type=jnp.float32)
    square_part = jnp.sum(wide_in * wide_in, axis=1)
    query_sum, key_sum, value_sum, square_sum = lax.psum(
        (query_part, key_part, value_part, square_part), "mp"
    )
    input_rms = jnp.sqrt(square_sum / D)
    inverse_rms = lax.rsqrt(square_sum / D + EPS)
    prompt_match = prompt_of[:, None] == jnp.arange(PROMPTS, dtype=jnp.int32)[None, :]
    prompt_start = jnp.sum(jnp.where(prompt_match, prompt_len[None, :], 0), axis=1)
    position = (
        (prompt_start + tail_len)[:, None] + jnp.arange(2, dtype=jnp.int32)[None, :]
    ).reshape(row_total)
    cosine, sine_table = rope_table(position, HD)
    query = apply_rope(
        (query_sum * inverse_rms[:, None]).reshape(row_total, head_local, HD), cosine, sine_table
    ).astype(jnp.bfloat16)
    key_new = apply_rope(
        (key_sum * inverse_rms[:, None]).reshape(row_total, kv_local, HD), cosine, sine_table
    ).astype(jnp.bfloat16)
    value_new = (
        (value_sum * inverse_rms[:, None]).astype(jnp.bfloat16).reshape(row_total, kv_local, HD)
    )
    row_first = model_index * (2 * req_local)
    own_keys = lax.dynamic_slice_in_dim(key_new, row_first, 2 * req_local, 0)
    own_values = lax.dynamic_slice_in_dim(value_new, row_first, 2 * req_local, 0)
    entries = jnp.concatenate([own_keys, own_values], axis=-1).reshape(
        req_local, 2, kv_local, 2 * HD
    )
    new_entries = jnp.transpose(entries, (0, 2, 1, 3))
    order = jnp.argsort(prompt_of, stable=True)
    inverse_order = jnp.argsort(order)
    query_grid = query.reshape(REQ, 2, kv_local, QPK, HD)
    grouped = query_grid[order].reshape(PROMPTS, CONT, 2, kv_local, QPK, HD)
    first_place = model_index * local_span
    highest, totals, accum = prompt_terms(grouped, prompt_cache, prompt_len, first_place)
    prompt_top = highest.reshape(REQ, 2, head_local)[inverse_order].reshape(row_total, head_local)
    prompt_total = totals.reshape(REQ, 2, head_local)[inverse_order].reshape(row_total, head_local)
    prompt_accum = accum.reshape(REQ, 2, head_local, HD)[inverse_order].reshape(
        row_total, head_local, HD
    )
    own_query = lax.dynamic_slice_in_dim(query_grid, model_index * req_local, req_local, 0)
    own_tail = lax.dynamic_slice_in_dim(tail_len, model_index * req_local, req_local, 0)
    tail_scores = (
        jnp.einsum(
            "ntgqd,ngjd->ntgqj", own_query, tail_cache[..., :HD], preferred_element_type=jnp.float32
        )
        * score_scale
    )
    tail_mask = (jnp.arange(tail_span, dtype=jnp.int32)[None, :] < own_tail[:, None])[
        :, None, None, None, :
    ]
    tail_top, tail_total, tail_weights = softmax_terms(tail_scores, tail_mask)
    tail_accum = jnp.einsum(
        "ntgqj,ngjd->ntgqd", tail_weights, tail_cache[..., HD:], preferred_element_type=jnp.float32
    )
    self_keys = own_keys.reshape(req_local, 2, kv_local, HD)
    self_values = own_values.reshape(req_local, 2, kv_local, HD)
    self_scores = (
        jnp.einsum("ntgqd,nugd->ntgqu", own_query, self_keys, preferred_element_type=jnp.float32)
        * score_scale
    )
    step_mask = (
        jnp.arange(2, dtype=jnp.int32)[None, :] <= jnp.arange(2, dtype=jnp.int32)[:, None]
    )[None, :, None, None, :]
    self_top, self_total, self_weights = softmax_terms(self_scores, step_mask)
    self_accum = jnp.einsum(
        "ntgqu,nugd->ntgqd", self_weights, self_values, preferred_element_type=jnp.float32
    )
    own_top, own_total, own_accum = merge_partials(
        (tail_top, tail_total, tail_accum), (self_top, self_total, self_accum)
    )
    full_top = lax.dynamic_update_slice_in_dim(
        jnp.full((row_total, head_local), NEG, jnp.float32),
        own_top.reshape(2 * req_local, head_local),
        row_first,
        0,
    )
    full_total = lax.dynamic_update_slice_in_dim(
        jnp.zeros((row_total, head_local), jnp.float32),
        own_total.reshape(2 * req_local, head_local),
        row_first,
        0,
    )
    full_accum = lax.dynamic_update_slice_in_dim(
        jnp.zeros((row_total, head_local, HD), jnp.float32),
        own_accum.reshape(2 * req_local, head_local, HD),
        row_first,
        0,
    )
    local_top, local_total, local_accum = merge_partials(
        (prompt_top, prompt_total, prompt_accum), (full_top, full_total, full_accum)
    )
    merged_top, merged_total, merged_accum = joined(
        (local_top, local_total, local_accum), "mp", merge_partials
    )
    attention = (
        (merged_accum / merged_total[..., None])
        .astype(jnp.bfloat16)
        .reshape(row_total, head_local * HD)
    )
    max_logit = jnp.max(merged_top.reshape(REQ, 2, head_local), axis=1)
    head_part = jnp.dot(attention, w_out, preferred_element_type=jnp.float32)
    own_row = (model_index * seq_count + seq_index) * row_share
    head_whole = lax.psum(head_part, "seq")
    residual = (wide_in + head_whole).astype(jnp.bfloat16)
    piece = lax.all_gather(residual, "mp", axis=1, tiled=True)
    wide_piece = piece.astype(jnp.float32)
    gain_piece = mlp_gain.astype(jnp.float32)
    scaled_piece = (wide_piece * gain_piece[None, :]).astype(jnp.bfloat16)
    gate_acc = jnp.dot(scaled_piece, w_gate, preferred_element_type=jnp.float32)
    up_acc = jnp.dot(scaled_piece, w_up, preferred_element_type=jnp.float32)
    square_acc = jnp.sum(wide_piece * wide_piece, axis=1)
    own_piece = lax.dynamic_slice_in_dim(piece, own_row, row_share, 0)
    own_block = own_piece
    gate_acc, up_acc, square_acc, own_block = (gate_acc, up_acc, square_acc, own_block)
    inverse_mid = lax.rsqrt(square_acc / D + EPS)
    gate_value = gate_acc * inverse_mid[:, None]
    up_value = up_acc * inverse_mid[:, None]
    hidden = (jax.nn.silu(gate_value) * up_value).astype(jnp.bfloat16)
    mlp_rows = lax.psum_scatter(
        jnp.dot(hidden, w_down, preferred_element_type=jnp.float32),
        ("mp", "seq"),
        scatter_dimension=0,
        tiled=True,
    )
    layer_out = (own_block.astype(jnp.float32) + mlp_rows).astype(jnp.bfloat16)
    return (layer_out, input_rms, max_logit, new_entries)


def solution(mesh):
    in_specs = (
        P(None, "mp"),
        P("mp"),
        P(),
        P("mp", "seq"),
        P("mp", "seq"),
        P("mp", "seq"),
        P("seq", "mp"),
        P(None, ("mp", "seq")),
        P(None, ("mp", "seq")),
        P(("mp", "seq"), None),
        P(None, "seq", "mp", None),
        P("mp", "seq", None, None),
        P(),
        P(),
        P(),
    )
    out_specs = (P(("mp", "seq"), None), P(), P(None, "seq"), P("mp", "seq", None, None))
    return jax.shard_map(shards, mesh=mesh, in_specs=in_specs, out_specs=out_specs, check_vma=False)
```

profile of v0, /device:TPU:0, one launch (start us, length us, event | category | flops | bytes accessed | tf_op | source)
XLA Modules:
  0.0 821.1 jit_solution(7491996693346277574)
XLA Ops:
  8.0 4.9 fusion.84
  15.5 2.5 sort.34
  18.1 2.5 sort.35
  20.8 24.3 %psum.36 = f32[256]{0:T(256)S(1)} all-reduce(f32[256]{0:T(256)S(1)} %fusion.68), channel_id=1, replica_groups=mesh['mp'=8,'seq'=4] {'mp'}, use_global_device_ids=true, to_apply=%region_2.0 | all-reduce | flops 256 | bytes 2048 | tf_op jit(solution)/shard_map/psum | solution.py:121
  46.4 88.4 %all-reduce.6.cloned.1.call-done = (f32[256,2048]{1,0:T(8,128)}, f32[256,256]{1,0:T(8,128)}, f32[256,256]{1,0:T(8,128)}) async-done(((f32[256,2048]{1,0:T(8,128)}, f32[256,256]{1,0:T(8,128)}, f32[256,256]{1,0:T(8,128)}), (f32[256,2048]{1,0:T(8,128)}, f32[256,256]{1,0:T(8,128)}, f32[256,256]{1,0:T(8,128)})) %all-reduce.6.cloned.1.call-update) | async-done | bytes 2621456 | tf_op jit(solution)/shard_map/psum | solution.py:121
  136.5 1.8 multiply_bitcast_fusion
  144.9 29.6 %bitcast_reduce_fusion = (f32[8,16,2,2,8]{4,2,1,3,0:T(2,128)S(1)}, f32[8,2,16,2,8,4096]{5,4,3,2,1,0:T(8,128)}) fusion(pred[8,4096]{1,0:T(8,128)(4,1)S(1)} %broadcast_compare_fusion, bf16[8,2,4096,256]{3,2,1,0:T(8,128)(2,1)} %param.27, bf16[8,16,2,2,8,128]{5,4,2,3,1,0:T(8,128)(2,1)} %bitcast.142), kind=kOutput, calls=%fused_computation.13 | convolution fusion | flops 4345294848 | bytes 84983808 | tf_op jit(solution)/shard_map/pntgqd,pgjd->pntgqj/dot_general | solution.py:74
  174.6 22.1 %fusion.6 = f32[8,16,2,2,8]{4,2,1,3,0:T(2,128)S(1)} fusion(f32[8,2,16,2,8,4096]{5,4,3,2,1,0:T(8,128)} %get-tuple-element.268, f32[8,16,2,2,8]{4,2,1,3,0:T(2,128)S(1)} %get-tuple-element.267, pred[8,4096]{1,0:T(8,128)(4,1)S(1)} %broadcast_compare_fusion), kind=kLoop, calls=%fused_computation.18 | loop fusion | flops 83881984 | bytes 67174400 | tf_op jit(solution)/shard_map/reduce_sum | solution.py:67
  196.8 30.3 %fusion.29 = f32[8,16,2,2,8,128]{5,4,2,1,3,0:T(8,128)} fusion(bf16[8,2,4096,256]{3,2,1,0:T(8,128)(2,1)} %param.27, f32[8,2,16,2,8,4096]{5,4,3,2,1,0:T(8,128)} %get-tuple-element.268, f32[8,16,2,2,8]{4,2,1,3,0:T(2,128)S(1)} %get-tuple-element.267, pred[8,4096]{1,0:T(8,128)(4,1)S(1)} %broadcast_compare_fusion), kind=kOutput, calls=%fused_computation.45 | convolution fusion | flops 4378853376 | bytes 86310912 | tf_op jit(solution)/shard_map/pntgqj,pgjd->pntgqd/dot_general | solution.py:80
  228.0 2.9 fusion.61
  233.5 3.2 copy.107
  236.7 2.3 gather_fusion.3
  239.3 2.8 fusion.28
  242.2 35.5 %all-gather = f32[2048,16]{1,0:T(8,128)S(1)} all-gather(f32[256,16]{1,0:T(8,128)S(1)} %get-tuple-element.246), channel_id=2, replica_groups=mesh['mp'=8,'seq'=4] {'mp'}, dimensions={0}, use_global_device_ids=true | all-gather | bytes 147456 | tf_op jit(solution)/shard_map/all_gather | solution.py:18
  277.8 36.8 %all-gather.1 = f32[2048,16]{1,0:T(8,128)S(1)} all-gather(f32[256,16]{1,0:T(8,128)S(1)} %get-tuple-element.243), channel_id=3, replica_groups=mesh['mp'=8,'seq'=4] {'mp'}, dimensions={0}, use_global_device_ids=true | all-gather | bytes 147456 | tf_op jit(solution)/shard_map/all_gather | solution.py:18
  315.4 169.6 %all-gather.8.cloned.1.call-done = f32[2048,16,128]{2,1,0:T(8,128)} async-done(((f32[256,16,128]{2,1,0:T(8,128)}), f32[2048,16,128]{2,1,0:T(8,128)}) %all-gather.8.cloned.1.call-update) | async-done | bytes 16777232 | tf_op jit(solution)/shard_map/all_gather | solution.py:18
  486.7 28.6 %while.19 = (s32[]{:T(128)}, f32[256,16]{0,1:T(8,128)S(1)}, f32[256,16]{0,1:T(8,128)S(1)}, f32[256,16,128]{2,1,0:T(8,128)S(1)}, f32[8,256,16]{1,2,0:T(8,128)S(1)...) while((s32[]{:T(128)}, f32[256,16]{0,1:T(8,128)S(1)}, ...), condition=%wide.region_15.16_spmd, body=%wide.region_14.15_spmd.sunk | while | flops 1597445 | bytes 6520983 | solution.py:23
  486.9 3.8 fusion.120
  491.0 3.8 fusion.120
  495.1 3.8 fusion.120
  499.2 3.8 fusion.120
  503.3 3.8 fusion.120
  507.4 3.8 fusion.120
  511.5 3.8 fusion.120
  516.2 4.5 fusion.70
  520.7 34.4 %all-reduce.4.cloned.1.call-done = f32[256,1024]{1,0:T(8,128)} async-done(((f32[256,1024]{1,0:T(8,128)}), f32[256,1024]{1,0:T(8,128)}) %all-reduce.4.cloned.1.call-update) | async-done | bytes 1048592 | tf_op jit(solution)/shard_map/psum | solution.py:222
  555.1 2.2 fusion.69
  557.4 73.8 %all-gather.6.cloned.1.call-done = bf16[256,8192]{1,0:T(8,128)(2,1)} async-done(((bf16[256,1024]{1,0:T(8,128)(2,1)}), bf16[256,8192]{1,0:T(8,128)(2,1)}) %all-gather.6.cloned.1.call-update) | async-done | bytes 4194320 | tf_op jit(solution)/shard_map/all_gather | solution.py:224
  631.2 3.3 fusion.17
  634.7 8.1 fusion.43
  642.8 22.7 %fusion.87 = f32[256,8192]{1,0:T(8,128)} fusion(bf16[896,8192]{1,0:T(8,128)(2,1)} %param.26, bf16[8192,896]{1,0:T(8,128)(2,1)} %param.25, bf16[256,8192]{1,0:T(8,128)(2,1)} %all-gather.6.cloned.1.call-done, f32[8192]{0:T(1024)S(1)} %convert_element_type.71, f32[256,896]{1,0:T(8,128)S(1)} %fusion.43, f32[256]{0:T(256)S(1)} %add_rsqrt_fusion), kind=kOutput, calls=%fused_computation.81 | convolution fusion | flops 7524089856 | bytes 42894336 | tf_op jit(solution)/shard_map/dot_general | solution.py:239
  667.9 145.0 %reduce-scatter.2.cloned.1.call-done = f32[8,8192]{1,0:T(8,128)} async-done(((f32[256,8192]{1,0:T(8,128)}), f32[8,8192]{1,0:T(8,128)}) %reduce-scatter.2.cloned.1.call-update) | async-done | bytes 262160 | tf_op jit(solution)/shard_map/reduce_scatter | solution.py:238
  (147 shorter events, 26.1 us)
Async XLA Ops:
  7.2 5.8 copy-start
  7.2 5.8 copy-start.2
  7.2 6.8 copy-start.6
  7.2 127.7 %all-reduce.6.cloned.1.call-start = ((), (), s32[]{:S(2)}) async-start(), calls=%async_computation.5 | async-start | bytes 5242880 | tf_op jit(solution)/shard_map/psum | solution.py:121
  12.9 2.2 copy-start.12
  13.0 2.2 copy-start.14
  13.0 2.3 copy-start.13
  15.1 469.9 %all-gather.8.cloned.1.call-start = ((), (), s32[]{:S(2)}) async-start(), calls=%async_computation.4 | async-start | bytes 18874368 | tf_op jit(solution)/shard_map/all_gather | solution.py:18
  138.3 2.9 slice-start
  138.7 3.2 slice-start.1
  140.4 0.7 copy-start.7
  227.1 3.9 copy-start.9
  242.2 312.9 %all-reduce.4.cloned.1.call-start = ((), (), s32[]{:S(2)}) async-start(), calls=%async_computation.1 | async-start | bytes 2097152 | tf_op jit(solution)/shard_map/psum | solution.py:222
  515.3 5.3 copy-start.4
  516.2 41.2 %copy-start.11 = (bf16[8192]{0:T(1024)(128)(2,1)S(1)}, bf16[8192]{0:T(1024)(128)(2,1)}, u32[]{:S(2)}) copy-start(bf16[8192]{0:T(1024)(128)(2,1)} %param.19) | copy-start | bytes 49156
  520.7 110.6 %all-gather.6.cloned.1.call-start = ((), (), s32[]{:S(2)}) async-start(), calls=%async_computation.2 | async-start | bytes 4718592 | tf_op jit(solution)/shard_map/all_gather | solution.py:224
  557.3 255.6 %reduce-scatter.2.cloned.1.call-start = ((), (), s32[]{:S(2)}) async-start(), calls=%async_computation.3 | async-start | bytes 8650752 | tf_op jit(solution)/shard_map/reduce_scatter | solution.py:238
  631.2 3.4 copy-start.3
  665.5 149.1 %copy-start.1 = (bf16[1024,256]{1,0:T(8,128)(2,1)S(1)}, bf16[1024,256]{1,0:T(8,128)(2,1)}, u32[]{:S(2)}) copy-start(bf16[1024,256]{1,0:T(8,128)(2,1)} %param.22) | copy-start | bytes 1572868
  665.5 0.8 copy-start.8
  665.5 0.8 copy-start.10
  665.5 1.5 copy-start.5
Sparse Core Ops, SparseCore 0:
  15.2 119.6 all-reduce.5
  242.3 242.5 all-gather.7
  520.8 34.2 all-reduce.3
  557.5 73.7 all-gather.5
  665.6 147.2 reduce-scatter.1
where the time goes:
time: 822 us; the launch traced here: 821 us
  waiting for transfers between devices  511 us (62%)
  matrix products  107 us (13%)
  blocking collectives  96.6 us (12%)
  other arithmetic  72.6 us (9%)
  local copies, waits for them, and re-layouts  18.4 us (2%)
  between operations  14.3 us (2%)
    all_gather x1, waiting for transfers between devices, joined(): gathered = jax.tree.map(lambda a: lax.all_gather(a, axis), part)  170 us
    reduce_scatter x1, waiting for transfers between devices, shards(): lax.psum_scatter(jnp.dot(hidden, w_down, preferred_element_type=jnp.float...  145 us
    psum x1, waiting for transfers between devices, shards(): lax.psum((query_part, key_part, value_part, square_part), 'mp')  88.4 us
    all_gather x1, waiting for transfers between devices, shards(): piece = lax.all_gather(residual, 'mp', axis=1, tiled=True)  73.8 us
    all_gather x2, blocking collectives, joined(): gathered = jax.tree.map(lambda a: lax.all_gather(a, axis), part)  72.4 us
    psum x1, waiting for transfers between devices, shards(): head_whole = lax.psum(head_part, 'seq')  34.4 us
    dot_general x1, matrix products, prompt_terms(): jnp.einsum('pntgqj,pgjd->pntgqd', weights, values_block, preferred_elemen...  30.3 us
    add x8, other arithmetic, merge_partials(): accum_early * factor_early[..., None] + accum_late * factor_late[..., None]  29.7 us
  transfers between devices with their start and end apart: 5, of which 5 were waited for; matrix products, arithmetic and copies ran while one was open for 1% of the time, Pallas kernels for 0%

commit v1 on v0

--- a/solution.py
+++ b/solution.py
@@ -221,7 +221,22 @@
     own_row = (model_index * seq_count + seq_index) * row_share
     head_whole = lax.psum(head_part, "seq")
     residual = (wide_in + head_whole).astype(jnp.bfloat16)
-    piece = lax.all_gather(residual, "mp", axis=1, tiled=True)
+
+    def _keep_up_masks(in_array, axis_key):
+        ndev = jax.lax.psum(1, axis_name=axis_key)
+        opened = sorted(((num, (num + 1) % ndev) for num in range(ndev)))
+        arr_now = in_array
+        buffers = [arr_now]
+        for jj in range(1, ndev):
+            arr_now = jax.lax.ppermute(arr_now, axis_name=axis_key, perm=opened)
+            buffers.insert(0, arr_now)
+        b_next = jnp.concatenate(buffers, 1)
+        low = jax.lax.axis_index(axis_key)
+        part_next = low + 1
+        g_now = jnp.roll(b_next, part_next * in_array.shape[1], 1)
+        return g_now
+
+    piece = _keep_up_masks(residual, "mp")
     wide_piece = piece.astype(jnp.float32)
     gain_piece = mlp_gain.astype(jnp.float32)
     scaled_piece = (wide_piece * gain_piece[None, :]).astype(jnp.bfloat16)

time: 822 us -> 844 us (1.027)
  waiting for transfers between devices: 511 us -> 529 us
    ppermute x0 -> x7, waiting for transfers between devices: none -> 94.7 us  [_keep_up_masks(): arr_now = jax.lax.ppermute(arr_now, axis_name=axis_key, perm=opened)]
    all_gather x1 -> x0, waiting for transfers between devices: 73.8 us -> none  [shards(): piece = lax.all_gather(residual, 'mp', axis=1, tiled=True)]
    dot_general x1, matrix products: 22.7 us -> 12 us  [shards(): jnp.dot(hidden, w_down, preferred_element_type=jnp.float32)]
  transfers between devices with their start and end apart: 5 -> 11, of which waited for: 5 -> 11; matrix products, arithmetic and copies ran while one was open for 1% -> 1% of each run, Pallas kernels for 0% -> 0%
where the time goes in v1:
time: 844 us; the launch traced here: 843 us
  waiting for transfers between devices  529 us (63%)
  matrix products  106 us (13%)
  blocking collectives  98.4 us (12%)
  other arithmetic  69.6 us (8%)
  local copies, waits for them, and re-layouts  23.2 us (3%)
  between operations  14.5 us (2%)
    all_gather x1, waiting for transfers between devices, joined(): gathered = jax.tree.map(lambda a: lax.all_gather(a, axis), part)  168 us
    reduce_scatter x1, waiting for transfers between devices, shards(): lax.psum_scatter(jnp.dot(hidden, w_down, preferred_element_type=jnp.float...  144 us
    ppermute x7, waiting for transfers between devices, _keep_up_masks(): arr_now = jax.lax.ppermute(arr_now, axis_name=axis_key, perm=opened)  94.7 us
    psum x1, waiting for transfers between devices, shards(): lax.psum((query_part, key_part, value_part, square_part), 'mp')  88.4 us
    all_gather x2, blocking collectives, joined(): gathered = jax.tree.map(lambda a: lax.all_gather(a, axis), part)  74.2 us
    psum x1, waiting for transfers between devices, shards(): head_whole = lax.psum(head_part, 'seq')  34.4 us
    dot_general x1, matrix products, prompt_terms(): jnp.einsum('pntgqj,pgjd->pntgqd', weights, values_block, preferred_elemen...  30.3 us
    add x8, other arithmetic, merge_partials(): accum_early * factor_early[..., None] + accum_late * factor_late[..., None]  29.7 us
  transfers between devices with their start and end apart: 11, of which 11 were waited for; matrix products, arithmetic and copies ran while one was open for 1% of the time, Pallas kernels for 0%

profile of v1, /device:TPU:0, one launch (start us, length us, event | category | flops | bytes accessed | tf_op | source)
XLA Modules:
  0.0 843.2 jit_solution(5780547213810019288)
XLA Ops:
  8.1 4.9 fusion.80
  23.0 24.3 %psum.36 = f32[256]{0:T(256)S(1)} all-reduce(f32[256]{0:T(256)S(1)} %fusion.62), channel_id=1, replica_groups=mesh['mp'=8,'seq'=4] {'mp'}, use_global_device_ids=true, to_apply=%region_2.0 | all-reduce | flops 256 | bytes 2048 | tf_op jit(solution)/shard_map/psum | solution.py:121
  48.6 88.4 %all-reduce.6.cloned.1.call-done = (f32[256,2048]{1,0:T(8,128)}, f32[256,256]{1,0:T(8,128)}, f32[256,256]{1,0:T(8,128)}) async-done(((f32[256,2048]{1,0:T(8,128)}, f32[256,256]{1,0:T(8,128)}, f32[256,256]{1,0:T(8,128)}), (f32[256,2048]{1,0:T(8,128)}, f32[256,256]{1,0:T(8,128)}, f32[256,256]{1,0:T(8,128)})) %all-reduce.6.cloned.1.call-update) | async-done | bytes 2621456 | tf_op jit(solution)/shard_map/psum | solution.py:121
  147.1 29.6 %bitcast_reduce_fusion = (f32[8,16,2,2,8]{4,2,1,3,0:T(2,128)S(1)}, f32[8,2,16,2,8,4096]{5,4,3,2,1,0:T(8,128)}) fusion(pred[8,4096]{1,0:T(8,128)(4,1)S(1)} %broadcast_compare_fusion, bf16[8,2,4096,256]{3,2,1,0:T(8,128)(2,1)} %param.27, bf16[8,16,2,2,8,128]{5,4,2,3,1,0:T(8,128)(2,1)} %bitcast.142), kind=kOutput, calls=%fused_computation.13 | convolution fusion | flops 4345294848 | bytes 84983808 | tf_op jit(solution)/shard_map/pntgqd,pgjd->pntgqj/dot_general | solution.py:74
  176.9 22.1 %fusion.6 = f32[8,16,2,2,8]{4,2,1,3,0:T(2,128)S(1)} fusion(f32[8,2,16,2,8,4096]{5,4,3,2,1,0:T(8,128)} %get-tuple-element.268, f32[8,16,2,2,8]{4,2,1,3,0:T(2,128)S(1)} %get-tuple-element.267, pred[8,4096]{1,0:T(8,128)(4,1)S(1)} %broadcast_compare_fusion), kind=kLoop, calls=%fused_computation.18 | loop fusion | flops 83881984 | bytes 67174400 | tf_op jit(solution)/shard_map/reduce_sum | solution.py:67
  199.0 30.3 %fusion.29 = f32[8,16,2,2,8,128]{5,4,2,1,3,0:T(8,128)} fusion(bf16[8,2,4096,256]{3,2,1,0:T(8,128)(2,1)} %param.27, f32[8,2,16,2,8,4096]{5,4,3,2,1,0:T(8,128)} %get-tuple-element.268, f32[8,16,2,2,8]{4,2,1,3,0:T(2,128)S(1)} %get-tuple-element.267, pred[8,4096]{1,0:T(8,128)(4,1)S(1)} %broadcast_compare_fusion), kind=kOutput, calls=%fused_computation.45 | convolution fusion | flops 4378853376 | bytes 86310912 | tf_op jit(solution)/shard_map/pntgqj,pgjd->pntgqd/dot_general | solution.py:80
  230.2 2.9 fusion.55
  235.7 3.2 copy.107
  244.4 35.5 %all-gather = f32[2048,16]{1,0:T(8,128)S(1)} all-gather(f32[256,16]{1,0:T(8,128)S(1)} %get-tuple-element.246), channel_id=2, replica_groups=mesh['mp'=8,'seq'=4] {'mp'}, dimensions={0}, use_global_device_ids=true | all-gather | bytes 147456 | tf_op jit(solution)/shard_map/all_gather | solution.py:18
  280.0 38.6 %all-gather.1 = f32[2048,16]{1,0:T(8,128)S(1)} all-gather(f32[256,16]{1,0:T(8,128)S(1)} %get-tuple-element.243), channel_id=3, replica_groups=mesh['mp'=8,'seq'=4] {'mp'}, dimensions={0}, use_global_device_ids=true | all-gather | bytes 147456 | tf_op jit(solution)/shard_map/all_gather | solution.py:18
  319.3 167.7 %all-gather.5.cloned.1.call-done = f32[2048,16,128]{2,1,0:T(8,128)} async-done(((f32[256,16,128]{2,1,0:T(8,128)}), f32[2048,16,128]{2,1,0:T(8,128)}) %all-gather.5.cloned.1.call-update) | async-done | bytes 16777232 | tf_op jit(solution)/shard_map/all_gather | solution.py:18
  488.7 28.6 %while.19 = (s32[]{:T(128)}, f32[256,16]{0,1:T(8,128)S(1)}, f32[256,16]{0,1:T(8,128)S(1)}, f32[256,16,128]{2,1,0:T(8,128)S(1)}, f32[8,256,16]{1,2,0:T(8,128)S(1)...) while((s32[]{:T(128)}, f32[256,16]{0,1:T(8,128)S(1)}, ...), condition=%wide.region_15.16_spmd, body=%wide.region_14.15_spmd.sunk | while | flops 1597445 | bytes 6520983 | solution.py:23
  489.0 3.8 fusion.115
  493.1 3.8 fusion.115
  497.2 3.8 fusion.115
  501.3 3.8 fusion.115
  505.3 3.8 fusion.115
  509.4 3.8 fusion.115
  513.5 3.8 fusion.115
  518.2 4.5 fusion.64
  522.8 34.4 %all-reduce.4.cloned.1.call-done = f32[256,1024]{1,0:T(8,128)} async-done(((f32[256,1024]{1,0:T(8,128)}), f32[256,1024]{1,0:T(8,128)}) %all-reduce.4.cloned.1.call-update) | async-done | bytes 1048592 | tf_op jit(solution)/shard_map/psum | solution.py:222
  560.1 14.7 %collective-permute-done = bf16[256,1024]{1,0:T(8,128)(2,1)S(1)} collective-permute-done((bf16[256,1024]{1,0:T(8,128)(2,1)S(1)}, bf16[256,1024]{1,0:T(8,128)(2,1)S(1)}, u32[]{:S(2)}, u32[]{:S(2)}) %collective-permute-start) | collective-permute-done | bytes 524320 | tf_op jit(solution)/shard_map/ppermute | solution.py:231
  574.7 15.2 %collective-permute-done.1 = bf16[256,1024]{1,0:T(8,128)(2,1)S(1)} collective-permute-done((bf16[256,1024]{1,0:T(8,128)(2,1)S(1)}, bf16[256,1024]{1,0:T(8,128)(2,1)S(1)}, u32[]{:S(2)}, u32[]{:S(2)}) %collective-permute-start.1) | collective-permute-done | bytes 524320 | tf_op jit(solution)/shard_map/ppermute | solution.py:231
  590.0 14.3 %collective-permute-done.2 = bf16[256,1024]{1,0:T(8,128)(2,1)S(1)} collective-permute-done((bf16[256,1024]{1,0:T(8,128)(2,1)S(1)}, bf16[256,1024]{1,0:T(8,128)(2,1)S(1)}, u32[]{:S(2)}, u32[]{:S(2)}) %collective-permute-start.2) | collective-permute-done | bytes 524320 | tf_op jit(solution)/shard_map/ppermute | solution.py:231
  604.3 13.4 %collective-permute-done.3 = bf16[256,1024]{1,0:T(8,128)(2,1)S(1)} collective-permute-done((bf16[256,1024]{1,0:T(8,128)(2,1)S(1)}, bf16[256,1024]{1,0:T(8,128)(2,1)S(1)}, u32[]{:S(2)}, u32[]{:S(2)}) %collective-permute-start.3) | collective-permute-done | bytes 524320 | tf_op jit(solution)/shard_map/ppermute | solution.py:231
  617.7 12.5 %collective-permute-done.4 = bf16[256,1024]{1,0:T(8,128)(2,1)S(1)} collective-permute-done((bf16[256,1024]{1,0:T(8,128)(2,1)S(1)}, bf16[256,1024]{1,0:T(8,128)(2,1)S(1)}, u32[]{:S(2)}, u32[]{:S(2)}) %collective-permute-start.4) | collective-permute-done | bytes 524320 | tf_op jit(solution)/shard_map/ppermute | solution.py:231
  630.2 12.4 %collective-permute-done.5 = bf16[256,1024]{1,0:T(8,128)(2,1)} collective-permute-done((bf16[256,1024]{1,0:T(8,128)(2,1)S(1)}, bf16[256,1024]{1,0:T(8,128)(2,1)}, u32[]{:S(2)}, u32[]{:S(2)}) %collective-permute-start.5) | collective-permute-done | bytes 524320 | tf_op jit(solution)/shard_map/ppermute | solution.py:231
  642.6 12.2 %collective-permute-done.6 = bf16[256,1024]{1,0:T(8,128)(2,1)} collective-permute-done((bf16[256,1024]{1,0:T(8,128)(2,1)}, bf16[256,1024]{1,0:T(8,128)(2,1)}, u32[]{:S(2)}, u32[]{:S(2)}) %collective-permute-start.6) | collective-permute-done | bytes 524320 | tf_op jit(solution)/shard_map/ppermute | solution.py:231
  660.6 11.1 %fusion.43 = f32[256,896]{1,0:T(8,128)S(1)} fusion(bf16[8192,896]{1,0:T(8,128)(2,1)} %param.24, f32[8192]{0:T(1024)S(1)} %convert_element_type.71, bf16[256,16384]{1,0:T(8,128)(2,1)S(1)} %constant_dynamic-update-slice_fusion, s32[]{:T(128)S(6)} %select_n.103, f32[256]{0:T(256)S(1)} %add_rsqrt_fusion), kind=kOutput, calls=%fused_computation.52 | convolution fusion | flops 3764617216 | bytes 19825668 | tf_op jit(solution)/shard_map/dot_general | solution.py:243
  672.1 4.5 fusion.46
  676.6 12.0 %fusion.74 = f32[256,8192]{1,0:T(8,128)} fusion(bf16[896,8192]{1,0:T(8,128)(2,1)} %param.26, f32[256,896]{1,0:T(8,128)S(1)} %fusion.46, f32[256,896]{1,0:T(8,128)S(1)} %fusion.43), kind=kOutput, calls=%fused_computation.77 | convolution fusion | flops 3759472640 | bytes 24903680 | tf_op jit(solution)/shard_map/dot_general | solution.py:254
  691.0 143.9 %reduce-scatter.2.cloned.1.call-done = f32[8,8192]{1,0:T(8,128)} async-done(((f32[256,8192]{1,0:T(8,128)}), f32[8,8192]{1,0:T(8,128)}) %reduce-scatter.2.cloned.1.call-update) | async-done | bytes 262160 | tf_op jit(solution)/shard_map/reduce_scatter | solution.py:253
  (174 shorter events, 48.9 us)
Async XLA Ops:
  7.2 5.8 copy-start
  7.2 15.7 %copy-start.2 = (bf16[256,1024]{1,0:T(8,128)(2,1)S(1)}, bf16[256,1024]{1,0:T(8,128)(2,1)}, u32[]{:S(2)}) copy-start(bf16[256,1024]{1,0:T(8,128)(2,1)} %param.17) | copy-start | bytes 1572868
  7.2 10.1 %copy-start.7 = (s32[8]{0:T(128)S(1)}, s32[8]{0:T(128)}, u32[]{:S(2)}) copy-start(s32[8]{0:T(128)} %param.29) | copy-start | bytes 100
  7.2 10.1 %copy-start.9 = (s32[128]{0:T(128)S(1)}, s32[128]{0:T(128)}, u32[]{:S(2)}) copy-start(s32[128]{0:T(128)} %param.31) | copy-start | bytes 1540
  7.2 10.2 %copy-start.8 = (s32[128]{0:T(128)S(1)}, s32[128]{0:T(128)}, u32[]{:S(2)}) copy-start(s32[128]{0:T(128)} %param.30) | copy-start | bytes 1540
  7.2 129.9 %all-reduce.6.cloned.1.call-start = ((), (), s32[]{:S(2)}) async-start(), calls=%async_computation.4 | async-start | bytes 5242880 | tf_op jit(solution)/shard_map/psum | solution.py:121
  17.3 469.7 %all-gather.5.cloned.1.call-start = ((), (), s32[]{:S(2)}) async-start(), calls=%async_computation.3 | async-start | bytes 18874368 | tf_op jit(solution)/shard_map/all_gather | solution.py:18
  140.5 2.9 slice-start
  140.9 3.2 slice-start.1
  142.6 0.7 copy-start.4
  244.4 312.8 %all-reduce.4.cloned.1.call-start = ((), (), s32[]{:S(2)}) async-start(), calls=%async_computation.1 | async-start | bytes 2097152 | tf_op jit(solution)/shard_map/psum | solution.py:222
  517.4 125.2 %copy-start.6 = (bf16[8192]{0:T(1024)(128)(2,1)S(1)}, bf16[8192]{0:T(1024)(128)(2,1)}, u32[]{:S(2)}) copy-start(bf16[8192]{0:T(1024)(128)(2,1)} %param.19) | copy-start | bytes 49156
  522.7 312.1 %reduce-scatter.2.cloned.1.call-start = ((), (), s32[]{:S(2)}) async-start(), calls=%async_computation.2 | async-start | bytes 8650752 | tf_op jit(solution)/shard_map/reduce_scatter | solution.py:253
  558.5 16.2 %collective-permute-start = (bf16[256,1024]{1,0:T(8,128)(2,1)S(1)}, bf16[256,1024]{1,0:T(8,128)(2,1)S(1)}, u32[]{:S(2)}, u32[]{:S(2)}) collective-permute-start(bf16[256,1024]{1,0:T(8,128)(2,1)S(1)} %fusion.63), channel_id=1, source_target_pairs={{0,4},{4,8},{8,12},{12,16},{16,20},{20,24},{24,28},{28,0},{1,5},{5... | collective-permute-start | bytes 1572872 | tf_op jit(solution)/shard_map/ppermute | solution.py:231
  574.7 15.2 %collective-permute-start.1 = (bf16[256,1024]{1,0:T(8,128)(2,1)S(1)}, bf16[256,1024]{1,0:T(8,128)(2,1)S(1)}, u32[]{:S(2)}, u32[]{:S(2)}) collective-permute-start(bf16[256,1024]{1,0:T(8,128)(2,1)S(1)} %collective-permute-done), channel_id=1, source_target_pairs={{0,4},{4,8},{8,12},{12,16},{16,20},{20,24},{24,28},{28,0},{1,5},{5... | collective-permute-start | bytes 1572872 | tf_op jit(solution)/shard_map/ppermute | solution.py:231
  590.0 14.3 %collective-permute-start.2 = (bf16[256,1024]{1,0:T(8,128)(2,1)S(1)}, bf16[256,1024]{1,0:T(8,128)(2,1)S(1)}, u32[]{:S(2)}, u32[]{:S(2)}) collective-permute-start(bf16[256,1024]{1,0:T(8,128)(2,1)S(1)} %collective-permute-done.1), channel_id=1, source_target_pairs={{0,4},{4,8},{8,12},{12,16},{16,20},{20,24},{24,28},{28,0},{1,5},{5... | collective-permute-start | bytes 1572872 | tf_op jit(solution)/shard_map/ppermute | solution.py:231
  604.3 13.4 %collective-permute-start.3 = (bf16[256,1024]{1,0:T(8,128)(2,1)S(1)}, bf16[256,1024]{1,0:T(8,128)(2,1)S(1)}, u32[]{:S(2)}, u32[]{:S(2)}) collective-permute-start(bf16[256,1024]{1,0:T(8,128)(2,1)S(1)} %collective-permute-done.2), channel_id=1, source_target_pairs={{0,4},{4,8},{8,12},{12,16},{16,20},{20,24},{24,28},{28,0},{1,5},{5... | collective-permute-start | bytes 1572872 | tf_op jit(solution)/shard_map/ppermute | solution.py:231
  617.7 12.5 %collective-permute-start.4 = (bf16[256,1024]{1,0:T(8,128)(2,1)S(1)}, bf16[256,1024]{1,0:T(8,128)(2,1)S(1)}, u32[]{:S(2)}, u32[]{:S(2)}) collective-permute-start(bf16[256,1024]{1,0:T(8,128)(2,1)S(1)} %collective-permute-done.3), channel_id=1, source_target_pairs={{0,4},{4,8},{8,12},{12,16},{16,20},{20,24},{24,28},{28,0},{1,5},{5... | collective-permute-start | bytes 1572872 | tf_op jit(solution)/shard_map/ppermute | solution.py:231
  630.2 12.4 %collective-permute-start.5 = (bf16[256,1024]{1,0:T(8,128)(2,1)S(1)}, bf16[256,1024]{1,0:T(8,128)(2,1)}, u32[]{:S(2)}, u32[]{:S(2)}) collective-permute-start(bf16[256,1024]{1,0:T(8,128)(2,1)S(1)} %collective-permute-done.4), channel_id=1, source_target_pairs={{0,4},{4,8},{8,12},{12,16},{16,20},{20,24},{24,28},{28,0},{1,5},{5... | collective-permute-start | bytes 1572872 | tf_op jit(solution)/shard_map/ppermute | solution.py:231
  642.6 12.2 %collective-permute-start.6 = (bf16[256,1024]{1,0:T(8,128)(2,1)}, bf16[256,1024]{1,0:T(8,128)(2,1)}, u32[]{:S(2)}, u32[]{:S(2)}) collective-permute-start(bf16[256,1024]{1,0:T(8,128)(2,1)} %collective-permute-done.5), channel_id=1, source_target_pairs={{0,4},{4,8},{8,12},{12,16},{16,20},{20,24},{24,28},{28,0},{1,5},{5... | collective-permute-start | bytes 1572872 | tf_op jit(solution)/shard_map/ppermute | solution.py:231
  659.6 12.2 %slice-start.2 = ((s8[14680064]{0:T(1024)(128)(4,1)}), s8[4194304]{0:T(1024)(128)(4,1)S(1)}, s32[]{:S(2)}) async-start(s8[14680064]{0:T(1024)(128)(4,1)} %bitcast.153), calls=%async_computation.7 | async-start | bytes 8388608
  659.7 12.1 %copy-start.3 = (bf16[256,16384]{1,0:T(8,128)(2,1)}, bf16[256,16384]{1,0:T(8,128)(2,1)S(1)}, u32[]{:S(2)}) copy-start(bf16[256,16384]{1,0:T(8,128)(2,1)S(1)} %constant_dynamic-update-slice_fusion) | copy-start | bytes 25165828
  660.6 11.2 %slice-start.3 = ((s8[14680064]{0:T(1024)(128)(4,1)}), s8[4194304]{0:T(1024)(128)(4,1)S(1)}, s32[]{:S(2)}) async-start(s8[14680064]{0:T(1024)(128)(4,1)} %bitcast.153), calls=%async_computation.8 | async-start | bytes 8388608
  660.6 11.2 %slice-start.4 = ((s8[14680064]{0:T(1024)(128)(4,1)}), s8[4194304]{0:T(1024)(128)(4,1)S(1)}, s32[]{:S(2)}) async-start(s8[14680064]{0:T(1024)(128)(4,1)} %bitcast.153), calls=%async_computation.9 | async-start | bytes 8388608
  660.6 11.4 %slice-start.5 = ((s8[14680064]{0:T(1024)(128)(4,1)}), s8[2097152]{0:T(1024)(128)(4,1)S(1)}, s32[]{:S(2)}) async-start(s8[14680064]{0:T(1024)(128)(4,1)} %bitcast.153), calls=%async_computation.10 | async-start | bytes 4194304
  676.6 160.0 %copy-start.1 = (bf16[1024,256]{1,0:T(8,128)(2,1)S(1)}, bf16[1024,256]{1,0:T(8,128)(2,1)}, u32[]{:S(2)}) copy-start(bf16[1024,256]{1,0:T(8,128)(2,1)} %param.22) | copy-start | bytes 1572868
  688.6 0.7 copy-start.5
Sparse Core Ops, SparseCore 0:
  17.4 119.6 all-reduce.5
  244.5 242.4 all-gather.4
  522.8 34.2 all-reduce.3
  688.8 146.0 reduce-scatter.1
